TPU v7x, 512 devices: a whole 4x4x16 slice. The times are simulated.
512 devices in a mesh: dp: 16 (over y, x), mp: 32 (over z, core).
Axes of the slice: x: 4, y: 4, z: 16, core: 2. Of those that a mesh axis runs over, the one named last changes fastest.
Arguments:
- act_cand: bfloat16 [1024, 4096], P('mp', 'dp'), may hold values from -6 to 6
- outgrad_cand: bfloat16 [1024, 16384], P('dp', 'mp'), may hold values from -6 to 6
- act_query: bfloat16 [512, 4096], P('mp', 'dp'), may hold values from -6 to 6
- outgrad_query: bfloat16 [512, 16384], P('dp', 'mp'), may hold values from -6 to 6
- loss_mask: int32 [16, 32], replicated, may hold values 0 or 1
- in_basis: bfloat16 [1024, 4096], P(None, 'dp'), may hold values from -0.1875 to 0.1875
- out_basis: bfloat16 [1024, 16384], P(None, 'mp'), may hold values from -0.1875 to 0.1875
- eigvals: float32 [4096, 16384], P('dp', 'mp'), may hold values from 0.05 to 5
Outputs:
- scores: float32 [16, 2], replicated
All inputs are finite; a program needn't handle non-finite values.
Results may differ from a plain program's by a relative error of at most 0.0048.
Values may be sent and summed in bfloat16 or wider, within the bound.
A program may use at most 64 MiB of HBM per device.

v0:
```python
import math

import jax
import jax.numpy as jnp
from jax import lax
from jax.sharding import PartitionSpec as P

DW = 4096
FW = 16384
BLK = 1024
QUERIES = 16
QLEN = 32
CLEN = 512
CANDS = 2


DAMPING = 0.1


def from_partner(block, axis, distance):
    count = lax.axis_size(axis)
    route = []
    for low in range(count):
        high = low | 1 << distance
        if high != low and high < count:
            route += [(low, high), (high, low)]
    return lax.ppermute(block, axis, route)


def rotate_blocks(wide, basis):
    tokens_here = wide.shape[0]
    block_width = basis.shape[0]
    nblocks = wide.shape[1] // block_width
    within = basis.shape[1] // nblocks
    turned = jnp.einsum(
        "tbk,kbj->tbj",
        wide.reshape(tokens_here, nblocks, block_width),
        basis.reshape(block_width, nblocks, within),
        preferred_element_type=jnp.float32,
    )
    return turned.reshape(tokens_here, basis.shape[1]).astype(jnp.bfloat16)


def join_pair(piece, partner, upper_half):
    front = jnp.where(upper_half, partner, piece)
    behind = jnp.where(upper_half, piece, partner)
    return jnp.concatenate([front, behind], 1)


def widen_input(piece):
    spread = max(BLK // piece.shape[1], 1)
    position = lax.axis_index("dp")
    for bit_number in range(spread.bit_length() - 1):
        partner = from_partner(piece, "dp", bit_number)
        upper_half = position // 2**bit_number % 2 == 1
        piece = join_pair(piece, partner, upper_half)
    return piece


def widen_output(piece):
    position = lax.axis_index("mp")
    partner = from_partner(piece, "mp", 0)
    upper_half = position // 2**0 % 2 == 1
    piece = join_pair(piece, partner, upper_half)
    return piece


def input_side(act_cand, act_query, in_basis):
    whole_cand, whole_query = (
        lax.all_gather(act_cand, "mp", axis=0, tiled=True),
        lax.all_gather(act_query, "mp", axis=0, tiled=True),
    )
    count_cand = whole_cand.shape[0]
    turned = rotate_blocks(widen_input(jnp.concatenate([whole_cand, whole_query], 0)), in_basis)
    return (turned[:count_cand], turned[count_cand:])


def output_side(outgrad_cand, outgrad_query, out_basis):
    whole_cand, whole_query = (
        lax.all_gather(outgrad_cand, "dp", axis=0, tiled=True),
        lax.all_gather(outgrad_query, "dp", axis=0, tiled=True),
    )
    count_cand = whole_cand.shape[0]
    turned = rotate_blocks(widen_output(jnp.concatenate([whole_cand, whole_query], 0)), out_basis)
    return (turned[:count_cand], turned[count_cand:])


def local(
    act_cand, outgrad_cand, act_query, outgrad_query, loss_mask, in_basis, out_basis, eigvals
):
    in_cand, in_query = input_side(act_cand, act_query, in_basis)
    out_cand, out_query = output_side(outgrad_cand, outgrad_query, out_basis)
    mask_rows = loss_mask.reshape(QUERIES * QLEN, 1).astype(jnp.bfloat16)
    masked = (in_query * mask_rows).reshape(QUERIES, QLEN, in_query.shape[1])
    query_grad = jnp.einsum(
        "qti,qtj->qij",
        masked,
        out_query.reshape(QUERIES, QLEN, out_query.shape[1]),
        preferred_element_type=jnp.float32,
    )
    precond = (query_grad / (eigvals + DAMPING)).astype(jnp.bfloat16)

    def one_query(single):
        applied = jnp.dot(in_cand, single, preferred_element_type=jnp.float32)
        return jnp.sum((applied * out_cand).reshape(CANDS, CLEN * applied.shape[1]), axis=1)

    partial_scores = lax.map(one_query, precond)
    summed = lax.psum(partial_scores, ("dp", "mp"))
    return summed * (1.0 / math.sqrt(QLEN * CLEN * DW * FW))


def solution(mesh):
    return jax.shard_map(
        local,
        mesh=mesh,
        in_specs=(
            P("mp", "dp"),
            P("dp", "mp"),
            P("mp", "dp"),
            P("dp", "mp"),
            P(),
            P(None, "dp"),
            P(None, "mp"),
            P("dp", "mp"),
        ),
        out_specs=P(),
        check_vma=False,
    )
```

profile of v0, /device:TPU:1, one launch (start us, length us, event | category | flops | bytes accessed | tf_op | source)
XLA Modules:
  0.0 321.2 jit_solution(5403024381032210717)
XLA Ops:
  6.5 39.4 %all_gather.12 = bf16[1024,256]{1,0:T(8,128)(2,1)S(1)} all-gather(bf16[32,256]{1,0:T(8,128)(2,1)} %param.10), channel_id=1, replica_groups=mesh['dp'=16,'mp'=32] {'mp'}, dimensions={0}, use_global_device_ids=true | all-gather | bytes 540672 | tf_op jit(solution)/shard_map/all_gather | solution.py:70
  45.9 27.8 %all_gather.13 = bf16[512,256]{1,0:T(8,128)(2,1)S(1)} all-gather(bf16[16,256]{1,0:T(8,128)(2,1)S(1)} %copy-done.3), channel_id=1, replica_groups=mesh['dp'=16,'mp'=32] {'mp'}, dimensions={0}, use_global_device_ids=true | all-gather | bytes 270336 | tf_op jit(solution)/shard_map/all_gather | solution.py:71
  73.8 3.1 collective-permute-start
  76.9 18.2 %collective-permute-done = bf16[1536,256]{1,0:T(8,128)(2,1)} collective-permute-done((bf16[1536,256]{1,0:T(8,128)(2,1)S(1)}, bf16[1536,256]{1,0:T(8,128)(2,1)}, u32[]{:S(2)}, u32[]{:S(2)}) %collective-permute-start) | collective-permute-done | bytes 786464 | tf_op jit(solution)/shard_map/ppermute | solution.py:27
  95.1 1.3 broadcast_select_fusion.5
  96.4 1.3 pad_maximum_fusion
  97.7 4.6 %collective-permute-start.1 = (bf16[1536,512]{1,0:T(8,128)(2,1)}, bf16[1536,512]{1,0:T(8,128)(2,1)}, u32[]{:S(2)}, u32[]{:S(2)}) collective-permute-start(bf16[1536,512]{1,0:T(8,128)(2,1)} %pad_maximum_fusion), channel_id=1, source_target_pairs={{0,64},{64,0},{32,96},{96,32},{128,192},{192,128},{160,224},{224,1... | collective-permute-start | bytes 4718600 | tf_op jit(solution)/shard_map/ppermute | solution.py:27
  102.3 48.3 %all_gather.15 = bf16[512,512]{1,0:T(8,128)(2,1)S(1)} all-gather(bf16[32,512]{1,0:T(8,128)(2,1)S(1)} %copy-done.2), channel_id=1, replica_groups=mesh['dp'=16,'mp'=32] {'dp'}, dimensions={0}, use_global_device_ids=true | all-gather | bytes 557056 | tf_op jit(solution)/shard_map/all_gather | solution.py:81
  150.6 10.2 %all-gather.2.cloned.1.call-done = bf16[1024,512]{1,0:T(8,128)(2,1)} async-done(((bf16[64,512]{1,0:T(8,128)(2,1)}), bf16[1024,512]{1,0:T(8,128)(2,1)}) %all-gather.2.cloned.1.call-update) | async-done | bytes 1048592 | tf_op jit(solution)/shard_map/all_gather | solution.py:80
  160.8 2.3 constant_dynamic-update-slice_fusion.3
  163.1 0.8 constant_dynamic-update-slice_fusion.2
  163.9 4.1 %collective-permute-start.2 = (bf16[1536,512]{1,0:T(8,128)(2,1)}, bf16[1536,512]{1,0:T(8,128)(2,1)}, u32[]{:S(2)}, u32[]{:S(2)}) collective-permute-start(bf16[1536,512]{1,0:T(8,128)(2,1)} %constant_dynamic-update-slice_fusion.2), channel_id=1, source_target_pairs={{0,1},{1,0},{2,3},{3,2},{4,5},{5,4},{6,7},{7,6},{8,9},{9,8},{10,11... | collective-permute-start | bytes 4718600 | tf_op jit(solution)/shard_map/ppermute | solution.py:27
  168.2 1.9 broadcast_add_fusion
  170.1 2.1 broadcast_select_fusion.3
  172.2 1.0 fusion.15
  173.2 0.1 slice_multiply_fusion
  173.3 0.7 copy-done.1
  174.1 2.1 broadcast_select_fusion.1
  176.2 1.9 fusion.12
  178.1 0.8 slice.17
  179.0 0.5 copy.11
  179.5 4.5 %divide_convert_fusion = bf16[16,256,512]{2,1,0:T(8,128)(2,1)} fusion(f32[256,512]{1,0:T(8,128)} %broadcast_add_fusion, bf16[16,32,256]{2,1,0:T(8,128)(2,1)S(1)} %bitcast.24, bf16[16,32,512]{2,1,0:T(8,128)(2,1)} %bitcast.23), kind=kOutput, calls=%fused_computation.5 | convolution fusion | flops 138412032 | bytes 5505024 | tf_op jit(solution)/shard_map/qti,qtj->qij/dot_general | solution.py:95
  184.0 26.1 %while.10 = (s32[]{:T(128)}, f32[16,2]{1,0:T(8,128)S(1)}, bf16[16,256,512]{2,1,0:T(8,128)(2,1)}, bf16[1024,256]{1,0:T(8,128)(2,1)S(1)}, bf16[1024,512]{0,1:T(8,128)(2,1)S(1)}, /*index=5*/s32[]{:T(128)}, f32[]{:T(128)}, s32[]{:T(128)}) while((s32[]{:T(128)}, f32[16,2]{1,0:T(8,128)S(1)}, bf16[16,256,512]{2,1,0:T(8,128)(2,1)}, ...), condition=%wide.region_3.4_spmd, body=%wide.region_0.3_spmd.sunk | while | flops 270008320 | bytes 1851521 | solution.py:107
  184.0 1.4 fusion.30
  185.5 0.1 reduce_sum.22
  185.7 1.4 fusion.30
  187.1 0.1 reduce_sum.22
  187.3 1.4 fusion.30
  188.8 0.1 reduce_sum.22
  188.9 1.4 fusion.30
  190.4 0.1 reduce_sum.22
  190.6 1.4 fusion.30
  192.2 1.4 fusion.30
  193.7 0.1 reduce_sum.22
  193.8 1.4 fusion.30
  195.3 0.1 reduce_sum.22
  195.5 1.4 fusion.30
  196.9 0.1 reduce_sum.22
  197.1 1.4 fusion.30
  198.7 1.4 fusion.30
  200.4 1.4 fusion.30
  202.0 1.4 fusion.30
  203.6 1.4 fusion.30
  205.3 1.4 fusion.30
  206.9 1.4 fusion.30
  208.5 1.4 fusion.30
  210.2 103.5 %psum.7 = f32[16,2]{0,1:T(2,128)S(1)} all-reduce(f32[16,2]{0,1:T(2,128)S(1)} %copy.12), channel_id=1, replica_groups=mesh['dp'=16,'mp'=32] {'dp','mp'}, use_global_device_ids=true, to_apply=%region_4.5 | all-reduce | flops 32 | bytes 256 | tf_op jit(solution)/shard_map/psum | solution.py:108
  313.7 0.6 broadcast_multiply_fusion
  (65 shorter events, 2.0 us)
Async XLA Ops:
  6.5 169.6 %copy-start = (bf16[1024,512]{1,0:T(8,128)(2,1)S(1)}, bf16[1024,512]{1,0:T(8,128)(2,1)}, u32[]{:S(2)}) copy-start(bf16[1024,512]{1,0:T(8,128)(2,1)} %param.16) | copy-start | bytes 3145732
  6.5 39.4 %copy-start.3 = (bf16[16,256]{1,0:T(8,128)(2,1)S(1)}, bf16[16,256]{1,0:T(8,128)(2,1)}, u32[]{:S(2)}) copy-start(bf16[16,256]{1,0:T(8,128)(2,1)} %param.12) | copy-start | bytes 24580
  6.5 154.3 %all-gather.2.cloned.1.call-start = ((), (), s32[]{:S(2)}) async-start(), calls=%async_computation | async-start | bytes 1114112 | tf_op jit(solution)/shard_map/all_gather | solution.py:80
  73.8 21.3 %collective-permute-start = (bf16[1536,256]{1,0:T(8,128)(2,1)S(1)}, bf16[1536,256]{1,0:T(8,128)(2,1)}, u32[]{:S(2)}, u32[]{:S(2)}) collective-permute-start(bf16[1536,256]{1,0:T(8,128)(2,1)S(1)} %constant_dynamic-update-slice_fusion), channel_id=1, source_target_pairs={{0,32},{32,0},{64,96},{96,64},{128,160},{160,128},{192,224},{224,1... | collective-permute-start | bytes 2359304 | tf_op jit(solution)/shard_map/ppermute | solution.py:27
  96.4 5.9 %copy-start.2 = (bf16[32,512]{1,0:T(8,128)(2,1)S(1)}, bf16[32,512]{1,0:T(8,128)(2,1)}, u32[]{:S(2)}) copy-start(bf16[32,512]{1,0:T(8,128)(2,1)} %param.13) | copy-start | bytes 98308
  97.7 72.5 %collective-permute-start.1 = (bf16[1536,512]{1,0:T(8,128)(2,1)}, bf16[1536,512]{1,0:T(8,128)(2,1)}, u32[]{:S(2)}, u32[]{:S(2)}) collective-permute-start(bf16[1536,512]{1,0:T(8,128)(2,1)} %pad_maximum_fusion), channel_id=1, source_target_pairs={{0,64},{64,0},{32,96},{96,32},{128,192},{192,128},{160,224},{224,1... | collective-permute-start | bytes 4718600 | tf_op jit(solution)/shard_map/ppermute | solution.py:27
  150.6 17.5 %copy-start.4 = (s32[16,32]{1,0:T(8,128)S(1)}, s32[16,32]{1,0:T(8,128)}, u32[]{:S(2)}) copy-start(s32[16,32]{1,0:T(8,128)} %param.14) | copy-start | bytes 6148
  163.9 10.1 %collective-permute-start.2 = (bf16[1536,512]{1,0:T(8,128)(2,1)}, bf16[1536,512]{1,0:T(8,128)(2,1)}, u32[]{:S(2)}, u32[]{:S(2)}) collective-permute-start(bf16[1536,512]{1,0:T(8,128)(2,1)} %constant_dynamic-update-slice_fusion.2), channel_id=1, source_target_pairs={{0,1},{1,0},{2,3},{3,2},{4,5},{5,4},{6,7},{7,6},{8,9},{9,8},{10,11... | collective-permute-start | bytes 4718600 | tf_op jit(solution)/shard_map/ppermute | solution.py:27
  170.1 2.1 copy-start.5
  173.2 0.9 copy-start.1
  179.5 4.5 %slice-start = ((bf16[1536,256]{1,0:T(8,128)(2,1)}), bf16[1024,256]{1,0:T(8,128)(2,1)S(1)}, s32[]{:S(2)}) async-start(bf16[1536,256]{1,0:T(8,128)(2,1)} %copy-done.1), calls=%async_computation.1 | async-start | bytes 1048576 | tf_op jit(solution)/shard_map/slice | solution.py:75
Sparse Core Ops, SparseCore 0:
  77.1 83.7 all-gather.1
where the time goes:
time: 322 us; the launch traced here: 321 us
  blocking collectives  219 us (68%)
  matrix products  30.5 us (9%)
  waiting for transfers between devices  28.4 us (9%)
  between operations  13.6 us (4%)
  starting transfers between devices  11.9 us (4%)
  other arithmetic  11.2 us (3%)
  local copies, waits for them, and re-layouts  6.16 us (2%)
    psum x1, blocking collectives, local(): summed = lax.psum(partial_scores, ('dp', 'mp'))  104 us
    all_gather x1, blocking collectives, output_side(): lax.all_gather(outgrad_query, 'dp', axis=0, tiled=True)  48.3 us
    all_gather x1, blocking collectives, input_side(): lax.all_gather(act_cand, 'mp', axis=0, tiled=True)  39.4 us
    all_gather x1, blocking collectives, input_side(): lax.all_gather(act_query, 'mp', axis=0, tiled=True)  27.8 us
    dot_general x16, matrix products, one_query(): applied = jnp.dot(in_cand, single, preferred_element_type=jnp.float32)  23.2 us
    ppermute x3, waiting for transfers between devices, from_partner(): return lax.ppermute(block, axis, route)  18.2 us
    ppermute x3, starting transfers between devices, from_partner(): return lax.ppermute(block, axis, route)  11.9 us
    all_gather x1, waiting for transfers between devices, output_side(): lax.all_gather(outgrad_cand, 'dp', axis=0, tiled=True)  10.2 us
  transfers between devices with their start and end apart: 4, of which 2 were waited for; matrix products, arithmetic and copies ran while one was open for 3% of the time, Pallas kernels for 0%

commit v1 on v0

v1 whole, which is shorter than its diff:
```python
import math

import jax
import jax.numpy as jnp
from jax import lax
from jax.experimental import pallas as pl
from jax.experimental.pallas import tpu as pltpu
from jax.sharding import PartitionSpec as P

DW = 4096
FW = 16384
QUERIES = 16
QLEN = 32
CLEN = 512
CANDS = 2
DAMPING = 0.1
SCALE = 1.0 / math.sqrt(QLEN * CLEN * DW * FW)

NX = 4
NZ = 16
CT, QT = 32, 16
CO, QO = 64, 32
WI, WO = 256, 512
HALF = (CO + QO) // 2

MESH = pl.DeviceIdType.MESH


def kernel(
    act_c, out_c, act_q, out_q, mask, in_basis, out_basis, eig,
    scores,
    actw, outw, basis_i, basis_o, eigv, maskv, maskcol, recip, in_all, out_all, part1, part2,
    load_sem, a_send, a_recv, b_send, b_recv, c_send, c_recv, pair_send, d_send, d_recv,
    e_send, e_recv, f_send, f_recv,
):
    dp = lax.axis_index("dp")
    mp = lax.axis_index("mp")
    y, x = dp // NX, dp % NX
    z, core = mp // 2, mp % 2
    partner = mp + 1 - 2 * core

    def at_z(step):
        return ((z + step + NZ) % NZ) * 2 + core

    def at_x(step):
        return y * NX + (x + step) % NX

    def at_y(step):
        return ((y + step) % NX) * NX + x

    def copy(src, dst, send, recv, to_dp, to_mp):
        return pltpu.make_async_remote_copy(
            src_ref=src, dst_ref=dst, send_sem=send, recv_sem=recv,
            device_id=(to_dp, to_mp), device_id_type=MESH,
        )

    loads = [
        pltpu.make_async_copy(act_c, actw.at[x, pl.ds(0, CT)], load_sem.at[0]),
        pltpu.make_async_copy(act_q, actw.at[x, pl.ds(CT, QT)], load_sem.at[1]),
        pltpu.make_async_copy(out_c, outw.at[core, pl.ds(0, CO)], load_sem.at[2]),
        pltpu.make_async_copy(out_q, outw.at[core, pl.ds(CO, QO)], load_sem.at[3]),
        pltpu.make_async_copy(out_basis, basis_o, load_sem.at[4]),
        pltpu.make_async_copy(in_basis, basis_i, load_sem.at[5]),
        pltpu.make_async_copy(mask, maskv, load_sem.at[6]),
        pltpu.make_async_copy(eig, eigv, load_sem.at[7]),
    ]

    barrier = pltpu.get_barrier_semaphore()
    greet = [(dp, partner)]
    greet += [(at_x(step), mp) for step in (1, 2, 3)]
    greet += [(at_y(step), mp) for step in (1, 2, 3)]
    greet += [(dp, at_z(step)) for step in (1, -1, 2, -2, 5, -5, 8)]
    for peer in greet:
        pl.semaphore_signal(barrier, inc=1, device_id=peer, device_id_type=MESH)
    for load in loads:
        load.start()
    for load in loads[:4]:
        load.wait()
    pl.semaphore_wait(barrier, len(greet))

    sends = []
    for step in (2, 1, 3):
        sends.append(copy(actw.at[x], actw.at[x], a_send.at[step], a_recv.at[step], at_x(step), mp))
    sends.append(copy(outw.at[core], outw.at[core], b_send, b_recv, dp, partner))
    for each in sends:
        each.start()

    loads[6].wait()
    rows = lax.broadcasted_iota(jnp.int32, (QLEN, QLEN), 0)
    lanes = lax.broadcasted_iota(jnp.int32, (QLEN, QLEN), 1)
    for q in range(QUERIES):
        spread = jnp.broadcast_to(maskv[pl.ds(q, 1), :].astype(jnp.float32), (QLEN, QLEN))
        column = jnp.sum(jnp.where(rows == lanes, spread, 0.0), axis=1, keepdims=True)
        maskcol[pl.ds(q * QLEN, QLEN), :] = jnp.broadcast_to(column, (QLEN, 128))
    loads[7].wait()
    recip[...] = 1.0 / (eigv[...] + DAMPING)

    loads[4].wait()
    sends[3].wait_recv()
    turned = jnp.dot(outw[0], basis_o[pl.ds(0, WO), :], preferred_element_type=jnp.float32)
    turned += jnp.dot(outw[1], basis_o[pl.ds(WO, WO), :], preferred_element_type=jnp.float32)
    out_all[dp] = turned.astype(jnp.bfloat16)

    def d_copy(half, slot, step, along_x, sem):
        rows = pl.ds(half * HALF, HALF)
        to_dp = at_x(step) if along_x else at_y(step)
        piece = out_all.at[slot, rows]
        return copy(piece, piece, d_send.at[sem], d_recv.at[half, slot], to_dp, mp)

    sem = 0
    for second in (False, True):
        for step in (2, 1, 3):
            for half in (0, 1):
                each = d_copy(half, dp, step, (half == 0) != second, sem)
                each.start()
                sends.append(each)
                sem += 1

    loads[5].wait()
    for each in sends[:3]:
        each.wait_recv()
    turned = jnp.dot(actw[0], basis_i[pl.ds(0, WI), :], preferred_element_type=jnp.float32)
    for piece in range(1, NX):
        turned += jnp.dot(
            actw[piece], basis_i[pl.ds(piece * WI, WI), :], preferred_element_type=jnp.float32
        )
    in_all[mp] = turned.astype(jnp.bfloat16)

    def c_copy(slot, step, sem):
        return copy(
            in_all.at[slot], in_all.at[slot], c_send.at[sem], c_recv.at[slot], dp, at_z(step)
        )

    def pair_copy(slot):
        return copy(
            in_all.at[slot], in_all.at[slot], pair_send.at[slot // 2], c_recv.at[slot], dp, partner
        )

    sem_c = 0
    for step in (8, 5, -5, 2, -2, 1, -1):
        each = c_copy(mp, step, sem_c)
        each.start()
        sends.append(each)
        sem_c += 1
    pair_copy(mp).start()

    for step in (1, 3, 2):
        for half in (0, 1):
            slot = at_x(step) if half == 0 else at_y(step)
            d_copy(half, slot, step, half == 0, 0).wait_recv()
            for onward in (2, 1, 3):
                each = d_copy(half, slot, onward, half == 1, sem)
                each.start()
                sends.append(each)
                sem += 1

    def arrive(step):
        slot = at_z(step)
        c_copy(slot, 1, 0).wait_recv()
        return slot

    for step in (1, -1, 2, -2):
        pair_copy(arrive(step)).start()
    for step in (5, -5):
        slot = arrive(step)
        for onward in (2, -2, 1, -1):
            each = c_copy(slot, onward, sem_c)
            each.start()
            sends.append(each)
            sem_c += 1
        pair_copy(slot).start()
    for step in (8, 4, -4, 6, -6, 3, -3, 7, -7):
        pair_copy(arrive(step)).start()

    for up in (1, 2, 3):
        for over in (1, 2, 3):
            slot = ((y + up) % NX) * NX + (x + over) % NX
            for half in (0, 1):
                d_copy(half, slot, 1, True, 0).wait_recv()
    for step in (1, 2, 3):
        d_copy(1, at_x(step), 1, True, 0).wait_recv()
        d_copy(0, at_y(step), 1, True, 0).wait_recv()

    def from_pair(step, carry):
        pair_copy(step * 2 + 1 - core).wait_recv()
        return carry

    lax.fori_loop(0, NZ, from_pair, 0)

    tokens = QUERIES * QLEN
    in_q = in_all[:, pl.ds(CT, QT), :].reshape(tokens, WI)
    folded = []
    for cand in range(CANDS):
        in_cand = in_all[pl.ds(cand * 16, 16), pl.ds(0, CT), :].reshape(CLEN, WI)
        out_cand = out_all[pl.ds(cand * 8, 8), pl.ds(0, CO), :].reshape(CLEN, WO)
        grad = lax.dot_general(
            in_cand, out_cand, (((0,), (0,)), ((), ())), preferred_element_type=jnp.float32
        )
        weight = (grad * recip[...]).astype(jnp.bfloat16)
        applied = jnp.dot(in_q, weight, preferred_element_type=jnp.float32)
        out_query = out_all[:, pl.ds(CO, QO), :].reshape(tokens, WO)
        product = applied * out_query.astype(jnp.float32)
        narrow = product[:, 0:128]
        for part in range(1, WO // 128):
            narrow += product[:, part * 128 : part * 128 + 128]
        narrow = narrow * maskcol[...]
        folded.append(jnp.sum(narrow.reshape(QUERIES, QLEN, 128), axis=1))
    column = jnp.sum(jnp.concatenate(folded, axis=0), axis=1, keepdims=True)
    count = QUERIES * CANDS
    rows = lax.broadcasted_iota(jnp.int32, (count, 128), 0)
    lanes = lax.broadcasted_iota(jnp.int32, (count, 128), 1)
    line = jnp.sum(
        jnp.where(rows == lanes, jnp.broadcast_to(column, (count, 128)), 0.0), axis=0, keepdims=True
    )

    flat = dp * 2 + core
    part1[flat] = line

    def e_copy(step):
        peer = (flat + step) % 32
        return copy(
            part1.at[flat], part1.at[flat], e_send.at[step], e_recv.at[step],
            peer // 2, z * 2 + peer % 2,
        )

    def e_start(step, carry):
        e_copy(step).start()
        return carry

    def e_wait(step, carry):
        e_copy(step).wait_recv()
        return carry

    lax.fori_loop(1, 32, e_start, 0)
    lax.fori_loop(1, 32, e_wait, 0)
    part2[z] = jnp.sum(part1[...], axis=0)

    def f_copy(step):
        return copy(
            part2.at[z], part2.at[z], f_send.at[step], f_recv.at[step], dp, at_z(step)
        )

    def f_start(step, carry):
        f_copy(step).start()
        return carry

    def f_wait(step, carry):
        f_copy(step).wait_recv()
        return carry

    lax.fori_loop(1, NZ, f_start, 0)
    lax.fori_loop(1, NZ, f_wait, 0)
    total = jnp.sum(part2[...], axis=0) * SCALE
    rows = lax.broadcasted_iota(jnp.int32, (QUERIES, 128), 0)
    lanes = lax.broadcasted_iota(jnp.int32, (QUERIES, 128), 1)
    spread = jnp.broadcast_to(total, (QUERIES, 128))
    for cand in range(CANDS):
        scores[:, pl.ds(cand, 1)] = jnp.sum(
            jnp.where(lanes == rows + cand * QUERIES, spread, 0.0), axis=1, keepdims=True
        )

    for each in sends:
        each.wait_send()

    def pair_sent(step, carry):
        pair_copy(step * 2 + core).wait_send()
        return carry

    lax.fori_loop(0, NZ, pair_sent, 0)

    def e_sent(step, carry):
        e_copy(step).wait_send()
        return carry

    lax.fori_loop(1, 32, e_sent, 0)

    def f_sent(step, carry):
        f_copy(step).wait_send()
        return carry

    lax.fori_loop(1, NZ, f_sent, 0)


def local(*args):
    dma = pltpu.SemaphoreType.DMA
    return pl.pallas_call(
        kernel,
        name="scores",
        out_shape=jax.ShapeDtypeStruct((QUERIES, CANDS), jnp.float32),
        in_specs=[pl.BlockSpec(memory_space=pl.ANY)] * 8,
        out_specs=pl.BlockSpec(memory_space=pltpu.VMEM),
        scratch_shapes=[
            pltpu.VMEM((NX, CT + QT, WI), jnp.bfloat16),
            pltpu.VMEM((2, CO + QO, WO), jnp.bfloat16),
            pltpu.VMEM((NX * WI, WI), jnp.bfloat16),
            pltpu.VMEM((2 * WO, WO), jnp.bfloat16),
            pltpu.VMEM((WI, WO), jnp.float32),
            pltpu.VMEM((QUERIES, QLEN), jnp.int32),
            pltpu.VMEM((QUERIES * QLEN, 128), jnp.float32),
            pltpu.VMEM((WI, WO), jnp.float32),
            pltpu.VMEM((2 * NZ, CT + QT, WI), jnp.bfloat16),
            pltpu.VMEM((NX * NX, CO + QO, WO), jnp.bfloat16),
            pltpu.VMEM((32, 1, 128), jnp.float32),
            pltpu.VMEM((NZ, 1, 128), jnp.float32),
            dma((8,)),
            dma((NX,)),
            dma((NX,)),
            dma,
            dma,
            dma((15,)),
            dma((2 * NZ,)),
            dma((NZ,)),
            dma((30,)),
            dma((2, NX * NX)),
            dma((32,)),
            dma((32,)),
            dma((NZ,)),
            dma((NZ,)),
        ],
        compiler_params=pltpu.CompilerParams(
            collective_id=0, has_side_effects=True, vmem_limit_bytes=48 << 20
        ),
    )(*args)


def solution(mesh):
    return jax.shard_map(
        local,
        mesh=mesh,
        in_specs=(
            P("mp", "dp"),
            P("dp", "mp"),
            P("mp", "dp"),
            P("dp", "mp"),
            P(),
            P(None, "dp"),
            P(None, "mp"),
            P("dp", "mp"),
        ),
        out_specs=P(),
        check_vma=False,
    )
```

time: 322 us -> 57.8 us (0.18)
  blocking collectives: 219 us -> 0 us
  Pallas kernels: 0 us -> 49.6 us
  matrix products: 30.5 us -> 0 us
  waiting for transfers between devices: 28.4 us -> 0 us
  between operations: 13.6 us -> 0.02 us
  starting transfers between devices: 11.9 us -> 0 us
  other arithmetic: 11.2 us -> 0 us
    all_gather x3 -> x0, blocking collectives: 115 us -> none  [the longest x1 48.3 us: output_side(): lax.all_gather(outgrad_query, 'dp', axis=0, tiled=True)]
    psum x1 -> x0, blocking collectives: 104 us -> none  [local(): summed = lax.psum(partial_scores, ('dp', 'mp'))]
    pallas_call x0 -> x1, Pallas kernels: none -> 49.6 us  [local(): pl.pallas_call(kernel, name='scores', out_shape=jax.ShapeDtypeStruct((QUE...]
    dot_general x19 -> x0, matrix products: 30.5 us -> none  [the longest x16 23.2 us: one_query(): applied = jnp.dot(in_cand, single, preferred_element_type=jnp.float32)]
    ppermute x3 -> x0, waiting for transfers between devices: 18.2 us -> none  [from_partner(): return lax.ppermute(block, axis, route)]
    ppermute x3 -> x0, starting transfers between devices: 11.9 us -> none  [from_partner(): return lax.ppermute(block, axis, route)]
    all_gather x1 -> x0, waiting for transfers between devices: 10.2 us -> none  [output_side(): lax.all_gather(outgrad_cand, 'dp', axis=0, tiled=True)]
    select_n x3 -> x0, other arithmetic: 5.4 us -> none  [join_pair(): front = jnp.where(upper_half, partner, piece)]
  transfers between devices with their start and end apart: 4 -> 0, of which waited for: 2 -> 0; matrix products, arithmetic and copies ran while one was open for 3% -> 0% of each run, Pallas kernels for 0% -> 0%
where the time goes in v1:
time: 57.8 us; the launch traced here: 57.3 us
  Pallas kernels  49.6 us (86%)
  local copies, waits for them, and re-layouts  7.65 us (13%)
    pallas_call x1, Pallas kernels, local(): pl.pallas_call(kernel, name='scores', out_shape=jax.ShapeDtypeStruct((QUE...  49.6 us
    unnamed x16, local copies, waits for them, and re-layouts  7.01 us

profile of v1, /device:TPU:1, one launch (start us, length us, event | category | flops | bytes accessed | tf_op | source)
XLA Modules:
  0.0 57.3 jit_solution(916098304234534498)
XLA Ops:
  0.0 0.0 copy-start
  0.0 1.2 %copy-done = bf16[1024,512]{1,0:T(8,128)(2,1)S(1)} copy-done((bf16[1024,512]{1,0:T(8,128)(2,1)S(1)}, bf16[1024,512]{1,0:T(8,128)(2,1)}, u32[]{:S(2)}) %copy-start) | copy-done | bytes 1048600
  1.2 0.0 copy-start.1
  1.2 1.0 %copy-done.1 = bf16[1024,256]{1,0:T(8,128)(2,1)S(1)} copy-done((bf16[1024,256]{1,0:T(8,128)(2,1)S(1)}, bf16[1024,256]{1,0:T(8,128)(2,1)}, u32[]{:S(2)}) %copy-start.1) | copy-done | bytes 524312
  2.3 0.0 copy-start.2
  2.3 1.0 %copy-done.2 = f32[256,512]{1,0:T(8,128)S(1)} copy-done((f32[256,512]{1,0:T(8,128)S(1)}, f32[256,512]{1,0:T(8,128)}, u32[]{:S(2)}) %copy-start.2) | copy-done | bytes 524312
  3.3 0.0 copy-start.3
  3.3 0.8 %copy-done.3 = bf16[64,512]{1,0:T(8,128)(2,1)S(1)} copy-done((bf16[64,512]{1,0:T(8,128)(2,1)S(1)}, bf16[64,512]{1,0:T(8,128)(2,1)}, u32[]{:S(2)}) %copy-start.3) | copy-done | bytes 65560
  4.2 0.0 copy-start.4
  4.2 0.8 %copy-done.4 = bf16[32,512]{1,0:T(8,128)(2,1)S(1)} copy-done((bf16[32,512]{1,0:T(8,128)(2,1)S(1)}, bf16[32,512]{1,0:T(8,128)(2,1)}, u32[]{:S(2)}) %copy-start.4) | copy-done | bytes 32792
  4.9 0.0 copy-start.5
  4.9 0.7 %copy-done.5 = bf16[32,256]{1,0:T(8,128)(2,1)S(1)} copy-done((bf16[32,256]{1,0:T(8,128)(2,1)S(1)}, bf16[32,256]{1,0:T(8,128)(2,1)}, u32[]{:S(2)}) %copy-start.5) | copy-done | bytes 16408
  5.6 0.0 copy-start.6
  5.6 0.7 %copy-done.6 = bf16[16,256]{1,0:T(8,128)(2,1)S(1)} copy-done((bf16[16,256]{1,0:T(8,128)(2,1)S(1)}, bf16[16,256]{1,0:T(8,128)(2,1)}, u32[]{:S(2)}) %copy-start.6) | copy-done | bytes 8216
  6.3 0.0 copy-start.7
  6.3 0.7 %copy-done.7 = s32[16,32]{1,0:T(8,128)S(1)} copy-done((s32[16,32]{1,0:T(8,128)S(1)}, s32[16,32]{1,0:T(8,128)}, u32[]{:S(2)}) %copy-start.7) | copy-done | bytes 2072
  7.0 49.6 %scores.1 = f32[16,2]{1,0:T(8,128)S(1)} custom-call(bf16[32,256]{1,0:T(8,128)(2,1)S(1)} %copy-done.5, bf16[64,512]{1,0:T(8,128)(2,1)S(1)} %copy-done.3, bf16[16,256]{1,0:T(8,128)(2,1)S(1)} %copy-done.6, bf16[32,512]{1,0:T(8,128)(2,1)S(1)} %copy-done.4, s32[16,32]{1,0:T(8,128)S(1)} %copy-done.7, bf16[1024,256]{1,0:T(8,128)(2,1)S(1)} %copy-done.1, ...), custom_call_target="tpu_custom_call" | custom-call | tf_op jit(solution)/shard_map/scores/pallas_call | solution.py:286
  56.7 0.6 %copy.9 = f32[16,2]{0,1:T(2,128)} copy(f32[16,2]{1,0:T(8,128)S(1)} %scores.1) | data formatting | bytes 256 | tf_op jit(solution)/shard_map/scores/pallas_call | solution.py:286
Async XLA Ops:
  0.0 1.2 %copy-start = (bf16[1024,512]{1,0:T(8,128)(2,1)S(1)}, bf16[1024,512]{1,0:T(8,128)(2,1)}, u32[]{:S(2)}) copy-start(bf16[1024,512]{1,0:T(8,128)(2,1)} %out_basis.1) | copy-start | bytes 3145732
  1.2 1.0 %copy-start.1 = (bf16[1024,256]{1,0:T(8,128)(2,1)S(1)}, bf16[1024,256]{1,0:T(8,128)(2,1)}, u32[]{:S(2)}) copy-start(bf16[1024,256]{1,0:T(8,128)(2,1)} %in_basis.1) | copy-start | bytes 1572868
  2.3 1.0 %copy-start.2 = (f32[256,512]{1,0:T(8,128)S(1)}, f32[256,512]{1,0:T(8,128)}, u32[]{:S(2)}) copy-start(f32[256,512]{1,0:T(8,128)} %eig.1) | copy-start | bytes 1572868
  3.3 0.8 %copy-start.3 = (bf16[64,512]{1,0:T(8,128)(2,1)S(1)}, bf16[64,512]{1,0:T(8,128)(2,1)}, u32[]{:S(2)}) copy-start(bf16[64,512]{1,0:T(8,128)(2,1)} %out_c.1) | copy-start | bytes 196612
  4.2 0.8 %copy-start.4 = (bf16[32,512]{1,0:T(8,128)(2,1)S(1)}, bf16[32,512]{1,0:T(8,128)(2,1)}, u32[]{:S(2)}) copy-start(bf16[32,512]{1,0:T(8,128)(2,1)} %out_q.1) | copy-start | bytes 98308
  4.9 0.7 %copy-start.5 = (bf16[32,256]{1,0:T(8,128)(2,1)S(1)}, bf16[32,256]{1,0:T(8,128)(2,1)}, u32[]{:S(2)}) copy-start(bf16[32,256]{1,0:T(8,128)(2,1)} %act_c.1) | copy-start | bytes 49156
  5.6 0.7 %copy-start.6 = (bf16[16,256]{1,0:T(8,128)(2,1)S(1)}, bf16[16,256]{1,0:T(8,128)(2,1)}, u32[]{:S(2)}) copy-start(bf16[16,256]{1,0:T(8,128)(2,1)} %act_q.1) | copy-start | bytes 24580
  6.3 0.7 %copy-start.7 = (s32[16,32]{1,0:T(8,128)S(1)}, s32[16,32]{1,0:T(8,128)}, u32[]{:S(2)}) copy-start(s32[16,32]{1,0:T(8,128)} %mask.1) | copy-start | bytes 6148

commit v2 on v1

--- a/solution.py
+++ b/solution.py
@@ -14,6 +14,12 @@
 CLEN = 512
 CANDS = 2
 DAMPING = 0.1
+FAR, NEAR = (5, -5), (2, -2, 1, -1)
+ONWARD = (2, 1, -1, -2)
+LAST = 3
+GREET = (2, -2, 1, -1)
+VOUCH = (2, 1)
+REST = (4, -4, 6, -6, 3, -3, 7, -7, 8)
 SCALE = 1.0 / math.sqrt(QLEN * CLEN * DW * FW)
 
 NX = 4
@@ -31,7 +37,7 @@
     scores,
     actw, outw, basis_i, basis_o, eigv, maskv, maskcol, recip, in_all, out_all, part1, part2,
     load_sem, a_send, a_recv, b_send, b_recv, c_send, c_recv, pair_send, d_send, d_recv,
-    e_send, e_recv, f_send, f_recv,
+    e_send, e_recv, f_send, f_recv, known,
 ):
     dp = lax.axis_index("dp")
     mp = lax.axis_index("mp")
@@ -66,24 +72,110 @@
     ]
 
     barrier = pltpu.get_barrier_semaphore()
-    greet = [(dp, partner)]
-    greet += [(at_x(step), mp) for step in (1, 2, 3)]
-    greet += [(at_y(step), mp) for step in (1, 2, 3)]
-    greet += [(dp, at_z(step)) for step in (1, -1, 2, -2, 5, -5, 8)]
+    greet = [(dp, at_z(step)) for step in GREET]
+    greet += [(at_x(step), mp) for step in (2, 1, 3)]
+    greet += [(at_y(step), mp) for step in (2, 1, 3)]
+    greet += [(dp, partner)]
     for peer in greet:
         pl.semaphore_signal(barrier, inc=1, device_id=peer, device_id_type=MESH)
     for load in loads:
         load.start()
-    for load in loads[:4]:
-        load.wait()
     pl.semaphore_wait(barrier, len(greet))
 
+    def vouch(level, reach):
+        for step in (reach, -reach):
+            pl.semaphore_signal(
+                known.at[level], inc=1, device_id=(dp, at_z(step)), device_id_type=MESH
+            )
+
     sends = []
+    a_copies = []
     for step in (2, 1, 3):
-        sends.append(copy(actw.at[x], actw.at[x], a_send.at[step], a_recv.at[step], at_x(step), mp))
-    sends.append(copy(outw.at[core], outw.at[core], b_send, b_recv, dp, partner))
+        for part, (src, first, count) in enumerate(((act_c, 0, CT), (act_q, CT, QT))):
+            a_copies.append(copy(
+                src, actw.at[x, pl.ds(first, count)], a_send.at[step, part], a_recv.at[step, part],
+                at_x(step), mp,
+            ))
+    b_copies = []
+    for part, (src, first, count) in enumerate(((out_c, 0, CO), (out_q, CO, QO))):
+        b_copies.append(copy(
+            src, outw.at[core, pl.ds(first, count)], b_send.at[part], b_recv.at[part], dp, partner
+        ))
+    sends += a_copies + b_copies
     for each in sends:
         each.start()
+    vouch(0, VOUCH[0])
+
+    for load in loads[2:5]:
+        load.wait()
+    for each in b_copies:
+        each.wait_recv()
+    turned = jnp.dot(outw[0], basis_o[pl.ds(0, WO), :], preferred_element_type=jnp.float32)
+    turned += jnp.dot(outw[1], basis_o[pl.ds(WO, WO), :], preferred_element_type=jnp.float32)
+    out_all[dp] = turned.astype(jnp.bfloat16)
+
+    def d_copy(half, slot, step, along_x, sem):
+        rows = pl.ds(half * HALF, HALF)
+        to_dp = at_x(step) if along_x else at_y(step)
+        piece = out_all.at[slot, rows]
+        return copy(piece, piece, d_send.at[sem], d_recv.at[half, slot], to_dp, mp)
+
+    sem_d = 0
+
+    def d_own(second):
+        nonlocal sem_d
+        for step in (2, 1, 3):
+            for half in (0, 1):
+                each = d_copy(half, dp, step, (half == 0) != second, sem_d)
+                each.start()
+                sends.append(each)
+                sem_d += 1
+
+    d_own(False)
+    for level, reach in enumerate(VOUCH[1:]):
+        pl.semaphore_wait(known.at[level], 2)
+        vouch(level + 1, reach)
+
+    for load in (loads[0], loads[1], loads[5]):
+        load.wait()
+    for each in a_copies:
+        each.wait_recv()
+    turned = jnp.dot(actw[0], basis_i[pl.ds(0, WI), :], preferred_element_type=jnp.float32)
+    for piece in range(1, NX):
+        turned += jnp.dot(
+            actw[piece], basis_i[pl.ds(piece * WI, WI), :], preferred_element_type=jnp.float32
+        )
+    in_all[mp] = turned.astype(jnp.bfloat16)
+
+    def c_copy(slot, step, sem):
+        return copy(
+            in_all.at[slot], in_all.at[slot], c_send.at[sem], c_recv.at[slot], dp, at_z(step)
+        )
+
+    def pair_copy(slot):
+        return copy(
+            in_all.at[slot], in_all.at[slot], pair_send.at[slot // 2], c_recv.at[slot], dp, partner
+        )
+
+    sem_c = 0
+
+    def c_out(slot, steps):
+        nonlocal sem_c
+        for step in steps:
+            each = c_copy(slot, step, sem_c)
+            each.start()
+            sends.append(each)
+            sem_c += 1
+
+    def arrive(step):
+        slot = at_z(step)
+        c_copy(slot, 1, 0).wait_recv()
+        return slot
+
+    pl.semaphore_wait(known.at[len(VOUCH) - 1], 2)
+    c_out(mp, FAR + NEAR)
+    pair_copy(mp).start()
+    d_own(True)
 
     loads[6].wait()
     rows = lax.broadcasted_iota(jnp.int32, (QLEN, QLEN), 0)
@@ -95,81 +187,25 @@
     loads[7].wait()
     recip[...] = 1.0 / (eigv[...] + DAMPING)
 
-    loads[4].wait()
-    sends[3].wait_recv()
-    turned = jnp.dot(outw[0], basis_o[pl.ds(0, WO), :], preferred_element_type=jnp.float32)
-    turned += jnp.dot(outw[1], basis_o[pl.ds(WO, WO), :], preferred_element_type=jnp.float32)
-    out_all[dp] = turned.astype(jnp.bfloat16)
-
-    def d_copy(half, slot, step, along_x, sem):
-        rows = pl.ds(half * HALF, HALF)
-        to_dp = at_x(step) if along_x else at_y(step)
-        piece = out_all.at[slot, rows]
-        return copy(piece, piece, d_send.at[sem], d_recv.at[half, slot], to_dp, mp)
-
-    sem = 0
-    for second in (False, True):
-        for step in (2, 1, 3):
-            for half in (0, 1):
-                each = d_copy(half, dp, step, (half == 0) != second, sem)
-                each.start()
-                sends.append(each)
-                sem += 1
-
-    loads[5].wait()
-    for each in sends[:3]:
-        each.wait_recv()
-    turned = jnp.dot(actw[0], basis_i[pl.ds(0, WI), :], preferred_element_type=jnp.float32)
-    for piece in range(1, NX):
-        turned += jnp.dot(
-            actw[piece], basis_i[pl.ds(piece * WI, WI), :], preferred_element_type=jnp.float32
-        )
-    in_all[mp] = turned.astype(jnp.bfloat16)
-
-    def c_copy(slot, step, sem):
-        return copy(
-            in_all.at[slot], in_all.at[slot], c_send.at[sem], c_recv.at[slot], dp, at_z(step)
-        )
-
-    def pair_copy(slot):
-        return copy(
-            in_all.at[slot], in_all.at[slot], pair_send.at[slot // 2], c_recv.at[slot], dp, partner
-        )
-
-    sem_c = 0
-    for step in (8, 5, -5, 2, -2, 1, -1):
-        each = c_copy(mp, step, sem_c)
-        each.start()
-        sends.append(each)
-        sem_c += 1
-    pair_copy(mp).start()
-
     for step in (1, 3, 2):
         for half in (0, 1):
             slot = at_x(step) if half == 0 else at_y(step)
             d_copy(half, slot, step, half == 0, 0).wait_recv()
             for onward in (2, 1, 3):
-                each = d_copy(half, slot, onward, half == 1, sem)
+                each = d_copy(half, slot, onward, half == 1, sem_d)
                 each.start()
                 sends.append(each)
-                sem += 1
-
-    def arrive(step):
-        slot = at_z(step)
-        c_copy(slot, 1, 0).wait_recv()
-        return slot
-
-    for step in (1, -1, 2, -2):
-        pair_copy(arrive(step)).start()
-    for step in (5, -5):
-        slot = arrive(step)
-        for onward in (2, -2, 1, -1):
-            each = c_copy(slot, onward, sem_c)
-            each.start()
-            sends.append(each)
-            sem_c += 1
-        pair_copy(slot).start()
-    for step in (8, 4, -4, 6, -6, 3, -3, 7, -7):
+                sem_d += 1
+
+    for step in FAR:
+        arrive(step)
+    c_out(at_z((2 * core - 1) * FAR[0]), (LAST - 2 * LAST * core,))
+    for onward in ONWARD:
+        for step in FAR:
+            c_out(at_z(step), (-onward if step > 0 else onward,))
+    for step in FAR:
+        pair_copy(at_z(step)).start()
+    for step in NEAR + REST:
         pair_copy(arrive(step)).start()
 
     for up in (1, 2, 3):
@@ -215,41 +251,42 @@
 
     flat = dp * 2 + core
     part1[flat] = line
-
-    def e_copy(step):
-        peer = (flat + step) % 32
-        return copy(
-            part1.at[flat], part1.at[flat], e_send.at[step], e_recv.at[step],
-            peer // 2, z * 2 + peer % 2,
-        )
-
-    def e_start(step, carry):
-        e_copy(step).start()
+    plane = [(up, over, other) for up in range(NX) for over in range(NX) for other in range(2)]
+    plane.sort(key=lambda o: (-min(o[0], NX - o[0]) - min(o[1], NX - o[1]), -o[2]))
+    plane.remove((0, 0, 0))
+    e_copies = []
+    for index, (up, over, other) in enumerate(plane):
+        to_dp = ((y + up) % NX) * NX + (x + over) % NX
+        to_core = (core + other) % 2
+        e_copies.append(copy(
+            part1.at[flat], part1.at[flat], e_send.at[index], e_recv.at[index],
+            to_dp, z * 2 + to_core,
+        ))
+    for each in e_copies:
+        each.start()
+    for each in reversed(e_copies):
+        each.wait_recv()
+    part2[z] = jnp.sum(part1[...], axis=0)
+
+    f_copies = []
+    for step in (8, 7, -7, 6, -6, 5, -5, 4, -4, 3, -3, 2, -2, 1, -1):
+        f_copies.append(copy(
+            part2.at[z], part2.at[z], f_send.at[step % NZ], f_recv.at[step % NZ], dp, at_z(step)
+        ))
+    for each in f_copies:
+        each.start()
+    for each in sends + e_copies:
+        each.wait_send()
+
+    def pair_sent(step, carry):
+        pair_copy(step * 2 + core).wait_send()
         return carry
 
-    def e_wait(step, carry):
-        e_copy(step).wait_recv()
-        return carry
-
-    lax.fori_loop(1, 32, e_start, 0)
-    lax.fori_loop(1, 32, e_wait, 0)
-    part2[z] = jnp.sum(part1[...], axis=0)
-
-    def f_copy(step):
-        return copy(
-            part2.at[z], part2.at[z], f_send.at[step], f_recv.at[step], dp, at_z(step)
-        )
-
-    def f_start(step, carry):
-        f_copy(step).start()
-        return carry
-
-    def f_wait(step, carry):
-        f_copy(step).wait_recv()
-        return carry
-
-    lax.fori_loop(1, NZ, f_start, 0)
-    lax.fori_loop(1, NZ, f_wait, 0)
+    lax.fori_loop(0, NZ, pair_sent, 0)
+    for each in f_copies:
+        each.wait_send()
+    for each in reversed(f_copies):
+        each.wait_recv()
     total = jnp.sum(part2[...], axis=0) * SCALE
     rows = lax.broadcasted_iota(jnp.int32, (QUERIES, 128), 0)
     lanes = lax.broadcasted_iota(jnp.int32, (QUERIES, 128), 1)
@@ -258,27 +295,6 @@
         scores[:, pl.ds(cand, 1)] = jnp.sum(
             jnp.where(lanes == rows + cand * QUERIES, spread, 0.0), axis=1, keepdims=True
         )
-
-    for each in sends:
-        each.wait_send()
-
-    def pair_sent(step, carry):
-        pair_copy(step * 2 + core).wait_send()
-        return carry
-
-    lax.fori_loop(0, NZ, pair_sent, 0)
-
-    def e_sent(step, carry):
-        e_copy(step).wait_send()
-        return carry
-
-    lax.fori_loop(1, 32, e_sent, 0)
-
-    def f_sent(step, carry):
-        f_copy(step).wait_send()
-        return carry
-
-    lax.fori_loop(1, NZ, f_sent, 0)
 
 
 def local(*args):
@@ -303,10 +319,10 @@
             pltpu.VMEM((32, 1, 128), jnp.float32),
             pltpu.VMEM((NZ, 1, 128), jnp.float32),
             dma((8,)),
-            dma((NX,)),
-            dma((NX,)),
-            dma,
-            dma,
+            dma((NX, 2)),
+            dma((NX, 2)),
+            dma((2,)),
+            dma((2,)),
             dma((15,)),
             dma((2 * NZ,)),
             dma((NZ,)),
@@ -316,9 +332,10 @@
             dma((32,)),
             dma((NZ,)),
             dma((NZ,)),
+            pltpu.SemaphoreType.REGULAR((3,)),
         ],
         compiler_params=pltpu.CompilerParams(
-            collective_id=0, has_side_effects=True, vmem_limit_bytes=48 << 20
+            collective_id=0, has_side_effects=True, vmem_limit_bytes=60 << 20
         ),
     )(*args)
 

time: 57.8 us -> 47.3 us (0.82)
  local copies, waits for them, and re-layouts: 7.65 us -> 1.33 us
  Pallas kernels: 49.6 us -> 45.8 us
    unnamed x16 -> x0, local copies, waits for them, and re-layouts: 7.01 us -> none
    pallas_call x1, Pallas kernels: 49.6 us -> 45.8 us  [local(): pl.pallas_call(kernel, name='scores', out_shape=jax.ShapeDtypeStruct((QUE...]
    pallas_call x1, local copies, waits for them, and re-layouts: 0.64 us -> 1.33 us  [local(): pl.pallas_call(kernel, name='scores', out_shape=jax.ShapeDtypeStruct((QUE...]
where the time goes in v2:
time: 47.3 us; the launch traced here: 47.1 us
  Pallas kernels  45.8 us (97%)
  local copies, waits for them, and re-layouts  1.33 us (3%)
    pallas_call x1, Pallas kernels, local(): pl.pallas_call(kernel, name='scores', out_shape=jax.ShapeDtypeStruct((QUE...  45.8 us
    pallas_call x1, local copies, waits for them, and re-layouts, local(): pl.pallas_call(kernel, name='scores', out_shape=jax.ShapeDtypeStruct((QUE...  1.33 us

profile of v2, /device:TPU:1, one launch (start us, length us, event | category | flops | bytes accessed | tf_op | source)
XLA Modules:
  0.0 47.1 jit_solution(11804573480913232582)
XLA Ops:
  0.0 45.8 %scores.1 = f32[16,2]{1,0:T(8,128)} custom-call(bf16[32,256]{1,0:T(8,128)(2,1)} %act_c.1, bf16[64,512]{1,0:T(8,128)(2,1)} %out_c.1, bf16[16,256]{1,0:T(8,128)(2,1)} %act_q.1, bf16[32,512]{1,0:T(8,128)(2,1)} %out_q.1, s32[16,32]{1,0:T(8,128)} %mask.1, bf16[1024,256]{1,0:T(8,128)(2,1)} %in_basis.1, bf16[1024,512]{1,0:T(8,128)(2,1)} %out_basis.1, f32[256,512]{1,0:T(8,128)} %eig.1), custom_call_target="tpu_custom_call" | custom-call | tf_op jit(solution)/shard_map/scores/pallas_call | solution.py:302
  45.8 1.3 %copy.9 = f32[16,2]{0,1:T(2,128)} copy(f32[16,2]{1,0:T(8,128)} %scores.1) | data formatting | bytes 256 | tf_op jit(solution)/shard_map/scores/pallas_call | solution.py:302

commit v3 on v2

--- a/solution.py
+++ b/solution.py
@@ -1,3 +1,4 @@
+import functools
 import math
 
 import jax
@@ -37,22 +38,26 @@
     scores,
     actw, outw, basis_i, basis_o, eigv, maskv, maskcol, recip, in_all, out_all, part1, part2,
     load_sem, a_send, a_recv, b_send, b_recv, c_send, c_recv, pair_send, d_send, d_recv,
-    e_send, e_recv, f_send, f_recv, known,
+    e_send, e_recv, f_send, f_recv, pair_recv, d_rest, known,
 ):
     dp = lax.axis_index("dp")
     mp = lax.axis_index("mp")
-    y, x = dp // NX, dp % NX
-    z, core = mp // 2, mp % 2
+    y, x = lax.div(dp, NX), lax.rem(dp, NX)
+    z, core = lax.div(mp, 2), lax.rem(mp, 2)
     partner = mp + 1 - 2 * core
 
     def at_z(step):
-        return ((z + step + NZ) % NZ) * 2 + core
+        return lax.rem(z + step + NZ, NZ) * 2 + core
+
+    @functools.cache
+    def in_plane(up, over):
+        return lax.rem(y + up, NX) * NX + lax.rem(x + over, NX)
 
     def at_x(step):
-        return y * NX + (x + step) % NX
+        return in_plane(0, step)
 
     def at_y(step):
-        return ((y + step) % NX) * NX + x
+        return in_plane(step, 0)
 
     def copy(src, dst, send, recv, to_dp, to_mp):
         return pltpu.make_async_remote_copy(
@@ -114,68 +119,20 @@
     turned += jnp.dot(outw[1], basis_o[pl.ds(WO, WO), :], preferred_element_type=jnp.float32)
     out_all[dp] = turned.astype(jnp.bfloat16)
 
-    def d_copy(half, slot, step, along_x, sem):
-        rows = pl.ds(half * HALF, HALF)
-        to_dp = at_x(step) if along_x else at_y(step)
-        piece = out_all.at[slot, rows]
-        return copy(piece, piece, d_send.at[sem], d_recv.at[half, slot], to_dp, mp)
-
-    sem_d = 0
-
-    def d_own(second):
-        nonlocal sem_d
+    def d_copy(half, slot, step, first):
+        to_dp = at_x(step) if (half == 0) == first else at_y(step)
+        part = out_all.at[slot, pl.ds(half * HALF, HALF)]
+        return copy(part, part, d_send, d_recv.at[half, step] if first else d_rest, to_dp, mp)
+
+    def d_own(first):
         for step in (2, 1, 3):
             for half in (0, 1):
-                each = d_copy(half, dp, step, (half == 0) != second, sem_d)
-                each.start()
-                sends.append(each)
-                sem_d += 1
-
-    d_own(False)
+                d_copy(half, dp, step, first).start()
+
+    d_own(True)
     for level, reach in enumerate(VOUCH[1:]):
         pl.semaphore_wait(known.at[level], 2)
         vouch(level + 1, reach)
-
-    for load in (loads[0], loads[1], loads[5]):
-        load.wait()
-    for each in a_copies:
-        each.wait_recv()
-    turned = jnp.dot(actw[0], basis_i[pl.ds(0, WI), :], preferred_element_type=jnp.float32)
-    for piece in range(1, NX):
-        turned += jnp.dot(
-            actw[piece], basis_i[pl.ds(piece * WI, WI), :], preferred_element_type=jnp.float32
-        )
-    in_all[mp] = turned.astype(jnp.bfloat16)
-
-    def c_copy(slot, step, sem):
-        return copy(
-            in_all.at[slot], in_all.at[slot], c_send.at[sem], c_recv.at[slot], dp, at_z(step)
-        )
-
-    def pair_copy(slot):
-        return copy(
-            in_all.at[slot], in_all.at[slot], pair_send.at[slot // 2], c_recv.at[slot], dp, partner
-        )
-
-    sem_c = 0
-
-    def c_out(slot, steps):
-        nonlocal sem_c
-        for step in steps:
-            each = c_copy(slot, step, sem_c)
-            each.start()
-            sends.append(each)
-            sem_c += 1
-
-    def arrive(step):
-        slot = at_z(step)
-        c_copy(slot, 1, 0).wait_recv()
-        return slot
-
-    pl.semaphore_wait(known.at[len(VOUCH) - 1], 2)
-    c_out(mp, FAR + NEAR)
-    pair_copy(mp).start()
-    d_own(True)
 
     loads[6].wait()
     rows = lax.broadcasted_iota(jnp.int32, (QLEN, QLEN), 0)
@@ -187,41 +144,73 @@
     loads[7].wait()
     recip[...] = 1.0 / (eigv[...] + DAMPING)
 
-    for step in (1, 3, 2):
-        for half in (0, 1):
-            slot = at_x(step) if half == 0 else at_y(step)
-            d_copy(half, slot, step, half == 0, 0).wait_recv()
-            for onward in (2, 1, 3):
-                each = d_copy(half, slot, onward, half == 1, sem_d)
-                each.start()
-                sends.append(each)
-                sem_d += 1
-
-    for step in FAR:
-        arrive(step)
-    c_out(at_z((2 * core - 1) * FAR[0]), (LAST - 2 * LAST * core,))
-    for onward in ONWARD:
-        for step in FAR:
-            c_out(at_z(step), (-onward if step > 0 else onward,))
+    for load in (loads[0], loads[1], loads[5]):
+        load.wait()
+    for each in a_copies:
+        each.wait_recv()
+    turned = jnp.dot(actw[0], basis_i[pl.ds(0, WI), :], preferred_element_type=jnp.float32)
+    for piece in range(1, NX):
+        turned += jnp.dot(
+            actw[piece], basis_i[pl.ds(piece * WI, WI), :], preferred_element_type=jnp.float32
+        )
+    in_all[mp] = turned.astype(jnp.bfloat16)
+
+    def c_copy(slot, step):
+        return copy(
+            in_all.at[slot], in_all.at[slot], c_send, c_recv.at[slot], dp, at_z(step)
+        )
+
+    def pair_copy(slot):
+        return copy(
+            in_all.at[slot], in_all.at[slot], pair_send, pair_recv, dp, partner
+        )
+
+    def c_out(slot, steps):
+        for step in steps:
+            c_copy(slot, step).start()
+
+    def arrive(step):
+        slot = at_z(step)
+        c_copy(slot, 1).wait_recv()
+        return slot
+
+    pl.semaphore_wait(known.at[len(VOUCH) - 1], 2)
+    c_out(mp, FAR + NEAR)
+    pair_copy(mp).start()
+    d_own(False)
+
+    def d_onward(steps):
+        for step in steps:
+            for half in (0, 1):
+                slot = at_x(step) if half == 0 else at_y(step)
+                d_copy(half, slot, NX - step, True).wait_recv()
+                for onward in (2, 1, 3):
+                    d_copy(half, slot, onward, False).start()
+
+    def c_onward(step):
+        slot = arrive(step)
+        for onward in ONWARD:
+            c_out(slot, (-onward if step > 0 else onward,))
+
+    def c_last():
+        c_out(at_z((2 * core - 1) * FAR[0]), (LAST - 2 * LAST * core,))
+
+    def c_pair(steps):
+        for step in steps:
+            pair_copy(arrive(step)).start()
+
+    d_onward((1, 3, 2))
+    c_onward(FAR[0])
+    c_onward(FAR[1])
+    c_last()
     for step in FAR:
         pair_copy(at_z(step)).start()
-    for step in NEAR + REST:
-        pair_copy(arrive(step)).start()
-
-    for up in (1, 2, 3):
-        for over in (1, 2, 3):
-            slot = ((y + up) % NX) * NX + (x + over) % NX
-            for half in (0, 1):
-                d_copy(half, slot, 1, True, 0).wait_recv()
-    for step in (1, 2, 3):
-        d_copy(1, at_x(step), 1, True, 0).wait_recv()
-        d_copy(0, at_y(step), 1, True, 0).wait_recv()
-
-    def from_pair(step, carry):
-        pair_copy(step * 2 + 1 - core).wait_recv()
-        return carry
-
-    lax.fori_loop(0, NZ, from_pair, 0)
+    c_pair(NEAR + REST)
+
+    rest = out_all.at[pl.ds(0, 12)]
+    pltpu.make_async_copy(rest, rest, d_rest).wait()
+    half_line = in_all.at[pl.ds(0, NZ)]
+    pltpu.make_async_copy(half_line, half_line, pair_recv).wait()
 
     tokens = QUERIES * QLEN
     in_q = in_all[:, pl.ds(CT, QT), :].reshape(tokens, WI)
@@ -256,37 +245,35 @@
     plane.remove((0, 0, 0))
     e_copies = []
     for index, (up, over, other) in enumerate(plane):
-        to_dp = ((y + up) % NX) * NX + (x + over) % NX
-        to_core = (core + other) % 2
         e_copies.append(copy(
-            part1.at[flat], part1.at[flat], e_send.at[index], e_recv.at[index],
-            to_dp, z * 2 + to_core,
+            part1.at[flat], part1.at[flat], e_send, e_recv,
+            in_plane(up, over), partner if other else mp,
         ))
     for each in e_copies:
         each.start()
-    for each in reversed(e_copies):
-        each.wait_recv()
+    others = part1.at[pl.ds(0, len(e_copies))]
+    pltpu.make_async_copy(others, others, e_recv).wait()
     part2[z] = jnp.sum(part1[...], axis=0)
 
     f_copies = []
     for step in (8, 7, -7, 6, -6, 5, -5, 4, -4, 3, -3, 2, -2, 1, -1):
         f_copies.append(copy(
-            part2.at[z], part2.at[z], f_send.at[step % NZ], f_recv.at[step % NZ], dp, at_z(step)
+            part2.at[z], part2.at[z], f_send, f_recv, dp, at_z(step)
         ))
     for each in f_copies:
         each.start()
-    for each in sends + e_copies:
+    for each in sends:
         each.wait_send()
-
-    def pair_sent(step, carry):
-        pair_copy(step * 2 + core).wait_send()
-        return carry
-
-    lax.fori_loop(0, NZ, pair_sent, 0)
-    for each in f_copies:
-        each.wait_send()
-    for each in reversed(f_copies):
-        each.wait_recv()
+    pltpu.make_async_copy(others, others, e_send).wait()
+    gone = in_all.at[pl.ds(0, NZ - 1)]
+    pltpu.make_async_copy(gone, gone, c_send).wait()
+    gone = out_all.at[pl.ds(0, 15)]
+    pltpu.make_async_copy(gone, gone, d_send).wait()
+
+    pltpu.make_async_copy(half_line, half_line, pair_send).wait()
+    others = part2.at[pl.ds(0, len(f_copies))]
+    pltpu.make_async_copy(others, others, f_send).wait()
+    pltpu.make_async_copy(others, others, f_recv).wait()
     total = jnp.sum(part2[...], axis=0) * SCALE
     rows = lax.broadcasted_iota(jnp.int32, (QUERIES, 128), 0)
     lanes = lax.broadcasted_iota(jnp.int32, (QUERIES, 128), 1)
@@ -323,15 +310,17 @@
             dma((NX, 2)),
             dma((2,)),
             dma((2,)),
-            dma((15,)),
+            dma,
             dma((2 * NZ,)),
-            dma((NZ,)),
-            dma((30,)),
-            dma((2, NX * NX)),
-            dma((32,)),
-            dma((32,)),
-            dma((NZ,)),
-            dma((NZ,)),
+            dma,
+            dma,
+            dma((2, NX)),
+            dma,
+            dma,
+            dma,
+            dma,
+            dma,
+            dma,
             pltpu.SemaphoreType.REGULAR((3,)),
         ],
         compiler_params=pltpu.CompilerParams(

time: 47.3 us -> 45.5 us (0.962)
  Pallas kernels: 45.8 us -> 44 us
    pallas_call x1, Pallas kernels: 45.8 us -> 44 us  [local(): pl.pallas_call(kernel, name='scores', out_shape=jax.ShapeDtypeStruct((QUE...]
where the time goes in v3:
time: 45.5 us; the launch traced here: 45.4 us
  Pallas kernels  44 us (97%)
  local copies, waits for them, and re-layouts  1.33 us (3%)
    pallas_call x1, Pallas kernels, local(): pl.pallas_call(kernel, name='scores', out_shape=jax.ShapeDtypeStruct((QUE...  44 us
    pallas_call x1, local copies, waits for them, and re-layouts, local(): pl.pallas_call(kernel, name='scores', out_shape=jax.ShapeDtypeStruct((QUE...  1.33 us

profile of v3, /device:TPU:1, one launch (start us, length us, event | category | flops | bytes accessed | tf_op | source)
XLA Modules:
  0.0 45.4 jit_solution(10280060340394413486)
XLA Ops:
  0.0 44.0 %scores.1 = f32[16,2]{1,0:T(8,128)} custom-call(bf16[32,256]{1,0:T(8,128)(2,1)} %act_c.1, bf16[64,512]{1,0:T(8,128)(2,1)} %out_c.1, bf16[16,256]{1,0:T(8,128)(2,1)} %act_q.1, bf16[32,512]{1,0:T(8,128)(2,1)} %out_q.1, s32[16,32]{1,0:T(8,128)} %mask.1, bf16[1024,256]{1,0:T(8,128)(2,1)} %in_basis.1, bf16[1024,512]{1,0:T(8,128)(2,1)} %out_basis.1, f32[256,512]{1,0:T(8,128)} %eig.1), custom_call_target="tpu_custom_call" | custom-call | tf_op jit(solution)/shard_map/scores/pallas_call | solution.py:289
  44.0 1.3 %copy.9 = f32[16,2]{0,1:T(2,128)} copy(f32[16,2]{1,0:T(8,128)} %scores.1) | data formatting | bytes 256 | tf_op jit(solution)/shard_map/scores/pallas_call | solution.py:289

commit v4 on v3

--- a/solution.py
+++ b/solution.py
@@ -83,7 +83,7 @@
     greet += [(dp, partner)]
     for peer in greet:
         pl.semaphore_signal(barrier, inc=1, device_id=peer, device_id_type=MESH)
-    for load in loads:
+    for load in loads[2:5]:
         load.start()
     pl.semaphore_wait(barrier, len(greet))
 
@@ -92,6 +92,8 @@
             pl.semaphore_signal(
                 known.at[level], inc=1, device_id=(dp, at_z(step)), device_id_type=MESH
             )
+
+    vouch(0, VOUCH[0])
 
     sends = []
     a_copies = []
@@ -109,7 +111,8 @@
     sends += a_copies + b_copies
     for each in sends:
         each.start()
-    vouch(0, VOUCH[0])
+    for load in loads[:2] + loads[5:]:
+        load.start()
 
     for load in loads[2:5]:
         load.wait()
@@ -189,11 +192,11 @@
 
     def c_onward(step):
         slot = arrive(step)
+        part = in_all.at[slot, pl.ds(CT, QT) if step > 0 else pl.ds(0, CT)]
+        away = at_z(-LAST if step > 0 else LAST)
+        copy(part, part, c_send, c_recv.at[slot], dp, away).start()
         for onward in ONWARD:
             c_out(slot, (-onward if step > 0 else onward,))
-
-    def c_last():
-        c_out(at_z((2 * core - 1) * FAR[0]), (LAST - 2 * LAST * core,))
 
     def c_pair(steps):
         for step in steps:
@@ -202,7 +205,6 @@
     d_onward((1, 3, 2))
     c_onward(FAR[0])
     c_onward(FAR[1])
-    c_last()
     for step in FAR:
         pair_copy(at_z(step)).start()
     c_pair(NEAR + REST)
@@ -275,21 +277,16 @@
     pltpu.make_async_copy(others, others, f_send).wait()
     pltpu.make_async_copy(others, others, f_recv).wait()
     total = jnp.sum(part2[...], axis=0) * SCALE
-    rows = lax.broadcasted_iota(jnp.int32, (QUERIES, 128), 0)
-    lanes = lax.broadcasted_iota(jnp.int32, (QUERIES, 128), 1)
-    spread = jnp.broadcast_to(total, (QUERIES, 128))
     for cand in range(CANDS):
-        scores[:, pl.ds(cand, 1)] = jnp.sum(
-            jnp.where(lanes == rows + cand * QUERIES, spread, 0.0), axis=1, keepdims=True
-        )
+        scores[pl.ds(cand, 1), :] = total[:, cand * QUERIES : cand * QUERIES + QUERIES]
 
 
 def local(*args):
     dma = pltpu.SemaphoreType.DMA
-    return pl.pallas_call(
+    by_cand = pl.pallas_call(
         kernel,
         name="scores",
-        out_shape=jax.ShapeDtypeStruct((QUERIES, CANDS), jnp.float32),
+        out_shape=pltpu.VMEM((CANDS, QUERIES), jnp.float32),
         in_specs=[pl.BlockSpec(memory_space=pl.ANY)] * 8,
         out_specs=pl.BlockSpec(memory_space=pltpu.VMEM),
         scratch_shapes=[
@@ -327,6 +324,7 @@
             collective_id=0, has_side_effects=True, vmem_limit_bytes=60 << 20
         ),
     )(*args)
+    return by_cand.T
 
 
 def solution(mesh):

time: 45.5 us -> 44 us (0.967)
  local copies, waits for them, and re-layouts: 1.33 us -> 0.56 us
  Pallas kernels: 44 us -> 43.3 us
    pallas_call x1 -> x0, local copies, waits for them, and re-layouts: 1.33 us -> none  [local(): pl.pallas_call(kernel, name='scores', out_shape=jax.ShapeDtypeStruct((QUE...]
    pallas_call x1, Pallas kernels: 44 us -> 43.3 us  [local(): pl.pallas_call(kernel, name='scores', out_shape=pltpu.VMEM((CANDS, QUERIE...]
    unnamed x0 -> x1, local copies, waits for them, and re-layouts: none -> 0.56 us
where the time goes in v4:
time: 44 us; the launch traced here: 43.9 us
  Pallas kernels  43.3 us (98%)
  local copies, waits for them, and re-layouts  0.56 us (1%)
    pallas_call x1, Pallas kernels, local(): pl.pallas_call(kernel, name='scores', out_shape=pltpu.VMEM((CANDS, QUERIE...  43.3 us

profile of v4, /device:TPU:1, one launch (start us, length us, event | category | flops | bytes accessed | tf_op | source)
XLA Modules:
  0.0 43.9 jit_solution(4374116552814211354)
XLA Ops:
  0.0 43.3 %scores.1 = f32[2,16]{1,0:T(2,128)S(1)} custom-call(bf16[32,256]{1,0:T(8,128)(2,1)} %act_c.1, bf16[64,512]{1,0:T(8,128)(2,1)} %out_c.1, bf16[16,256]{1,0:T(8,128)(2,1)} %act_q.1, bf16[32,512]{1,0:T(8,128)(2,1)} %out_q.1, s32[16,32]{1,0:T(8,128)} %mask.1, bf16[1024,256]{1,0:T(8,128)(2,1)} %in_basis.1, bf16[1024,512]{1,0:T(8,128)(2,1)} %out_basis.1, ...), custom_call_target="tpu_custom_call" | custom-call | tf_op jit(solution)/shard_map/scores/pallas_call | solution.py:286
  43.3 0.6 %copy.10 = f32[16,2]{0,1:T(2,128)} copy(f32[16,2]{0,1:T(2,128)S(1)} %bitcast.1) | data formatting | bytes 256

commit v5 on v4

--- a/solution.py
+++ b/solution.py
@@ -15,12 +15,12 @@
 CLEN = 512
 CANDS = 2
 DAMPING = 0.1
-FAR, NEAR = (5, -5), (2, -2, 1, -1)
-ONWARD = (2, 1, -1, -2)
-LAST = 3
+FAR, NEAR = (4, -4), (3, -3, 2, -2, 1, -1)
+ONWARD = (3, 2, 1)
+LAST = 4
 GREET = (2, -2, 1, -1)
-VOUCH = (2, 1)
-REST = (4, -4, 6, -6, 3, -3, 7, -7, 8)
+VOUCH = (2,)
+REST = (5, -5, 6, -6, 7, -7, 8)
 SCALE = 1.0 / math.sqrt(QLEN * CLEN * DW * FW)
 
 NX = 4

time: 44 us -> 43.9 us (level)
  no operation moved by 1% of the time
where the time goes in v5:
time: 43.9 us; the launch traced here: 43.7 us
  Pallas kernels  43.1 us (98%)
  local copies, waits for them, and re-layouts  0.56 us (1%)
    pallas_call x1, Pallas kernels, local(): pl.pallas_call(kernel, name='scores', out_shape=pltpu.VMEM((CANDS, QUERIE...  43.1 us

profile of v5, /device:TPU:1, one launch (start us, length us, event | category | flops | bytes accessed | tf_op | source)
XLA Modules:
  0.0 43.7 jit_solution(14785996170368310524)
XLA Ops:
  0.0 43.1 %scores.1 = f32[2,16]{1,0:T(2,128)S(1)} custom-call(bf16[32,256]{1,0:T(8,128)(2,1)} %act_c.1, bf16[64,512]{1,0:T(8,128)(2,1)} %out_c.1, bf16[16,256]{1,0:T(8,128)(2,1)} %act_q.1, bf16[32,512]{1,0:T(8,128)(2,1)} %out_q.1, s32[16,32]{1,0:T(8,128)} %mask.1, bf16[1024,256]{1,0:T(8,128)(2,1)} %in_basis.1, bf16[1024,512]{1,0:T(8,128)(2,1)} %out_basis.1, ...), custom_call_target="tpu_custom_call" | custom-call | tf_op jit(solution)/shard_map/scores/pallas_call | solution.py:286
  43.2 0.6 %copy.10 = f32[16,2]{0,1:T(2,128)} copy(f32[16,2]{0,1:T(2,128)S(1)} %bitcast.1) | data formatting | bytes 256
